TPU v7x, 128 devices: a whole 4x4x4 slice. The times are simulated.
128 devices in a mesh: row: 8 (over z, y_hi), col: 16 (over x, y_lo, core).
Axes of the slice: x: 4, y: 4 (y_hi: 2, y_lo: 2; y = y_hi * 2 + y_lo), z: 4, core: 2. Of those that a mesh axis runs over, the one named last changes fastest.
Arguments:
- amplitudes: bfloat16 [10000, 4096], P('row', 'col'), may hold values from -6 to 6
- integrals: bfloat16 [4096, 16384], P(('row', 'col')), may hold values from -0.09375 to 0.09375
- storage_slot: int32 [4096], P('row'), may hold values from 0 to 4095, as said below
Outputs:
- ladder: float32 [10000, 16384], P(None, ('col', 'row'))
Inputs may be any that keep to these rules, and one draw needn't show every extreme that they name: storage_slot is a permutation of 0 to 4095 that keeps every index k within its own aligned block of 4096 // 8 indices.
All inputs are finite; a program needn't handle non-finite values.
Results may differ from a plain program's by a relative error of at most 0.0003.
Values may be sent and summed in bfloat16 or wider, within the bound.
A program may use at most 64 MiB of HBM per device.

v0:
```python
import jax
import jax.numpy as jnp
from jax import lax
from jax.sharding import PartitionSpec as P


def shards(amplitudes, integrals, storage_slot):
    moved_rows = lax.all_to_all(integrals, "col", split_axis=1, concat_axis=0, tiled=True)
    block_rows = moved_rows.shape[0]
    local_slot = storage_slot - lax.axis_index("row") * block_rows
    ordered = jnp.take(moved_rows, local_slot, axis=0)
    int_whole = lax.all_gather(ordered, "row", axis=0, tiled=True)
    ladder = jnp.dot(
        lax.all_gather(amplitudes, "col", axis=1, tiled=True),
        int_whole,
        preferred_element_type=jnp.float32,
    )
    return lax.all_to_all(ladder, "row", split_axis=1, concat_axis=0, tiled=True)


def solution(mesh):
    in_specs = (P("row", "col"), P(("row", "col"), None), P("row"))
    out_specs = P(None, ("col", "row"))
    return jax.shard_map(shards, mesh=mesh, in_specs=in_specs, out_specs=out_specs, check_vma=False)
```

profile of v0, /device:TPU:1, one launch (start us, length us, event | category | flops | bytes accessed | tf_op | source)
XLA Modules:
  0.0 306.8 jit_solution(8422305112034208156)
XLA Ops:
  6.5 2.3 copy.11
  8.8 6.8 %all-to-all-start = ((bf16[32,16,1024]{2,0,1:T(8,128)(2,1)}), bf16[32,16,1024]{2,0,1:T(8,128)(2,1)S(1)}, u32[]{:S(2)}, u32[]{:S(2)}) async-start(bf16[32,16,1024]{2,0,1:T(8,128)(2,1)} %bitcast.13), calls=%async_computation | async-start | bytes 2097152 | tf_op jit(solution)/shard_map/all_to_all | solution.py:8
  15.7 0.0 all-gather.3.cloned.1.call-start
  15.7 0.7 compare_and_fusion
  16.4 15.0 %all-to-all-done = bf16[32,16,1024]{2,0,1:T(8,128)(2,1)S(1)} async-done(((bf16[32,16,1024]{2,0,1:T(8,128)(2,1)}), bf16[32,16,1024]{2,0,1:T(8,128)(2,1)S(1)}, u32[]{:S(2)}, u32[]{:S(2)}) %all-to-all-start) | async-done | bytes 1048608 | tf_op jit(solution)/shard_map/all_to_all | solution.py:8
  31.4 2.0 gather_fusion
  33.4 1.1 broadcast_select_fusion
  34.6 0.0 all-gather.3.cloned.1.call-update
  34.6 0.0 all-gather.5.cloned.1.call-start
  34.6 0.7 all-gather.5.cloned.1.call-update
  35.3 106.8 %all-gather.3.cloned.1.call-done = bf16[4096,1024]{1,0:T(8,128)(2,1)} async-done(((bf16[512,1024]{1,0:T(8,128)(2,1)}), bf16[4096,1024]{1,0:T(8,128)(2,1)}) %all-gather.3.cloned.1.call-update) | async-done | bytes 8388624 | tf_op jit(solution)/shard_map/all_gather | solution.py:12
  142.1 69.6 %all-gather.5.cloned.1.call-done = bf16[1250,4096]{1,0:T(8,128)(2,1)} async-done(((bf16[1250,256]{1,0:T(8,128)(2,1)}), bf16[1250,4096]{1,0:T(8,128)(2,1)}) %all-gather.5.cloned.1.call-update) | async-done | bytes 10240016 | tf_op jit(solution)/shard_map/all_gather | solution.py:14
  211.7 15.5 %fusion = f32[1024,1250]{0,1:T(8,128)S(1)} fusion(bf16[4096,1024]{1,0:T(8,128)(2,1)} %all-gather.3.cloned.1.call-done, bf16[1250,4096]{1,0:T(8,128)(2,1)} %all-gather.5.cloned.1.call-done), kind=kOutput, calls=%fused_computation.6 | convolution fusion | flops 10485760000 | bytes 23748608 | tf_op jit(solution)/shard_map/dot_general | solution.py:13
  227.2 1.3 copy.9
  228.5 0.4 slice.2
  228.9 1.0 copy.7
  229.9 65.9 %all_to_all.38 = f32[1250,8,128]{2,0,1:T(8,128)} all-to-all(f32[1250,8,128]{2,0,1:T(8,128)S(1)} %copy.7), channel_id=1, replica_groups=mesh['row'=8,'col'=16] {'row'}, dimensions={1} | all-to-all | bytes 10240000 | tf_op jit(solution)/shard_map/all_to_all | solution.py:18
  295.7 4.2 %all_to_all.35 = f32[10000,128]{1,0:T(8,128)} reshape(f32[8,1250,128]{2,1,0:T(8,128)} %bitcast.15) | data formatting | bytes 10240000 | tf_op jit(solution)/shard_map/all_to_all | solution.py:18
  (1 shorter events, 0.0 us)
Async XLA Ops:
  8.8 22.5 %all-to-all-start = ((bf16[32,16,1024]{2,0,1:T(8,128)(2,1)}), bf16[32,16,1024]{2,0,1:T(8,128)(2,1)S(1)}, u32[]{:S(2)}, u32[]{:S(2)}) async-start(bf16[32,16,1024]{2,0,1:T(8,128)(2,1)} %bitcast.13), calls=%async_computation | async-start | bytes 2097152 | tf_op jit(solution)/shard_map/all_to_all | solution.py:8
  15.7 126.4 %all-gather.3.cloned.1.call-start = ((), (), s32[]{:S(2)}) async-start(), calls=%async_computation.2 | async-start | bytes 9437184 | tf_op jit(solution)/shard_map/all_gather | solution.py:12
  34.6 177.1 %all-gather.5.cloned.1.call-start = ((), (), s32[]{:S(2)}) async-start(), calls=%async_computation.3 | async-start | bytes 10932224 | tf_op jit(solution)/shard_map/all_gather | solution.py:14
Sparse Core Ops, SparseCore 0:
  34.7 107.3 all-gather.2
  143.7 67.9 all-gather.4
where the time goes:
time: 307 us
  waiting for transfers between devices  192 us (63%)
  blocking collectives  65.9 us (21%)
  matrix products  15.5 us (5%)
  between operations  13.5 us (4%)
  local copies, waits for them, and re-layouts  11.2 us (4%)
  starting transfers between devices  6.91 us (2%)
    all_gather x1, waiting for transfers between devices, shards(): int_whole = lax.all_gather(ordered, 'row', axis=0, tiled=True)  107 us
    all_gather x1, waiting for transfers between devices, shards(): lax.all_gather(amplitudes, 'col', axis=1, tiled=True)  69.6 us
    all_to_all x1, blocking collectives, shards(): lax.all_to_all(ladder, 'row', split_axis=1, concat_axis=0, tiled=True)  65.9 us
    dot_general x1, matrix products, shards(): jnp.dot(lax.all_gather(amplitudes, 'col', axis=1, tiled=True), int_whole,...  15.5 us
    all_to_all x1, waiting for transfers between devices, shards(): lax.all_to_all(integrals, 'col', split_axis=1, concat_axis=0, tiled=True)  15 us
    all_to_all x1, starting transfers between devices, shards(): lax.all_to_all(integrals, 'col', split_axis=1, concat_axis=0, tiled=True)  6.83 us
  transfers between devices with their start and end apart: 3, of which 3 were waited for; matrix products, arithmetic and copies ran while one was open for 0% of the time, Pallas kernels for 0%

commit v1 on v0

v1 whole, which is shorter than its diff:
```python
import functools

import jax
import jax.numpy as jnp
from jax import lax
from jax.experimental import pallas as pl
from jax.experimental.pallas import tpu as pltpu
from jax.sharding import PartitionSpec as P

MESH = pl.DeviceIdType.MESH
T = 128
TILES = 5
HALF = T * TILES
LIFT = 2.0**40
TOP = 32767.0


def device(x, y, z, k):
    return (z * 2 + y // 2, (x * 2 + y % 2) * 2 + k)


def wait(ref, sem):
    pltpu.make_async_copy(ref, ref, sem).wait()


def ladder_kernel(
    a_ref, i_ref, slot_ref, q_ref, m_ref,
    apad, lhs, onehot, slots, ipack, amp, ints, codes, tops,
    slot_send, slot_recv, half_send, half_recv, own_sem,
    plane_send, plane_recv, line_send, line_recv, pair_send, pair_recv,
    amp_send, amp_recv, out_send, out_recv, top_send, top_recv,
):
    row, col = lax.axis_index("row"), lax.axis_index("col")
    x, y, z, k = col // 4, (row % 2) * 2 + (col // 2) % 2, row // 2, col % 2
    block = col // 2
    me = (row % 2) * 8 + block

    def chip_of(p):
        return (p % 8) // 2, (p // 8) * 2 + p % 2

    def place(px, py):
        return (py // 2) * 8 + px * 2 + py % 2

    barrier = pltpu.get_barrier_semaphore()

    def greet(d):
        pl.semaphore_signal(barrier, inc=1, device_id=d, device_id_type=MESH)

    for d in range(1, 16):
        px, py = chip_of(me ^ d)
        greet(device(px, py, z, k))
    for d in range(1, 4):
        for c in range(2):
            greet(device(x, y, (z + d) % 4, c))
    greet(device(x, y, z, 1 - k))
    mirrored = row != block

    @pl.when(mirrored)
    def _():
        greet((block, 2 * row + k))

    def pack(p, _):
        px, py = chip_of(p)
        base = (px * 2 + py % 2) * 16 + py // 2
        for zz in range(4):
            for c in range(2):
                at = pl.multiple_of((base + c * 8 + zz * 2) * 128, 128)
                ipack[p, :, (zz * 2 + c) * 128 : (zz * 2 + c + 1) * 128] = i_ref[:, pl.ds(at, 128)]
        return _

    lax.fori_loop(0, 16, pack, None)
    rows = a_ref.shape[0]
    low = rows // 16 * 16
    apad[low:, :] = jnp.zeros((2 * HALF - low, 256), jnp.bfloat16)
    apad[0:rows, :] = a_ref[...]

    def ints_row(zs, p):
        return pl.multiple_of(((zs * 2 + p // 8) * 2 + k) * 256 + (p % 8) * 32, 32)

    mine = pl.ds(ints_row(z, me), 32)
    ints[mine, :] = ipack[me]

    pl.semaphore_wait(barrier, 22 + mirrored.astype(jnp.int32))

    def slot_copy():
        return pltpu.make_async_remote_copy(
            slot_ref, slots, slot_send, slot_recv, device_id=(block, 2 * row + k), device_id_type=MESH
        )

    half_copy = pltpu.make_async_remote_copy(
        apad.at[pl.ds(pl.multiple_of((1 - k) * HALF, HALF), HALF)],
        lhs.at[:, pl.ds(pl.multiple_of(k * 256, 256), 256)],
        half_send, half_recv, device_id=device(x, y, z, 1 - k), device_id_type=MESH,
    )

    @pl.when(mirrored)
    def _():
        slot_copy().start()

    half_copy.start()

    def line_copy(zs, p, to):
        part = ints.at[pl.ds(ints_row(zs, p), 32)]
        pltpu.make_async_remote_copy(
            part, part, line_send, line_recv.at[zs * 16 + p], device_id=device(x, y, to, k), device_id_type=MESH
        ).start()

    def line_wait(zs, p):
        wait(ints.at[pl.ds(ints_row(zs, p), 32)], line_recv.at[zs * 16 + p])

    up, down, far = (z + 1) % 4, (z + 3) % 4, (z + 2) % 4

    def plane_out(d, _):
        p = me ^ d
        px, py = chip_of(p)
        pltpu.make_async_remote_copy(
            ipack.at[p], ints.at[mine], plane_send, plane_recv.at[me],
            device_id=device(px, py, z, k), device_id_type=MESH,
        ).start()
        return _

    lax.fori_loop(1, 16, plane_out, None)
    line_copy(z, me, up)
    line_copy(z, me, down)

    own = pltpu.make_async_copy(
        apad.at[pl.ds(pl.multiple_of(k * HALF, HALF), HALF)],
        lhs.at[:, pl.ds(pl.multiple_of(k * 256, 256), 256)],
        own_sem,
    )
    own.start()

    @pl.when(mirrored)
    def _():
        slot_copy().wait()

    @pl.when(jnp.logical_not(mirrored))
    def _():
        slots[...] = slot_ref[...]

    def mark(s, _):
        at = lax.broadcasted_iota(jnp.int32, (64, 512), 0) + s * 64
        stored = ((at % 256) // 32) * 64 + (at // 256) * 32 + at % 32
        hit = (slots[0:1, :] - block * 512) == stored
        onehot[pl.ds(pl.multiple_of(s * 64, 64), 64), :] = jnp.where(hit, 1.0, 0.0).astype(jnp.bfloat16)
        return _

    lax.fori_loop(0, 8, mark, None)
    half_copy.wait()
    own.wait()

    def amp_rows(t, yhi):
        return pl.ds(pl.multiple_of((t * 2 + yhi) * T, T), T)

    def order(t, _):
        part = lax.dot_general(
            lhs[pl.ds(pl.multiple_of(t * T, T), T), :], onehot[...], (((1,), (1,)), ((), ())),
            preferred_element_type=jnp.float32,
        )
        amp[amp_rows(t, row % 2), pl.ds(pl.multiple_of(block * 512, 512), 512)] = part.astype(jnp.bfloat16)
        return _

    lax.fori_loop(0, TILES, order, None)

    def piece(t, px, py, c):
        return amp.at[
            amp_rows(t, py // 2),
            pl.ds(pl.multiple_of(((px * 2 + py % 2) * 2 + c) * 256, 256), 256),
        ]

    def at(u, v, c):
        fx, fy = (u, v) if c == 0 else (v, u)
        return (x + fx) % 4, (y + fy) % 4

    def amp_sem(t, px, py, c):
        return amp_recv.at[(t * 16 + place(px, py)) * 2 + c]

    def send(t, src, c, to):
        part = piece(t, *src, c)
        pltpu.make_async_remote_copy(
            part, part, amp_send.at[t], amp_sem(t, *src, c), device_id=device(*to, z, k), device_id_type=MESH
        ).start()

    def arrive(t, src, c):
        wait(piece(t, *src, c), amp_sem(t, *src, c))

    def when(cond):
        return pl.when(cond) if not isinstance(cond, bool) else (lambda f: f() if cond else None)

    def first(t):
        for c in range(2):
            for s in (1, 3):
                send(t, at(0, 0, c), c, at(s, 0, c))

    def spread(t, src, c):
        for s in (1, 3):
            send(t, src, c, at(0, s, c))

    def second(t):
        for c in range(2):
            spread(t, at(0, 0, c), c)
            for s in (1, 3):
                arrive(t, at(s, 0, c), c)
                spread(t, at(s, 0, c), c)
            go = 1 + 2 * ((t + c) % 2)
            send(t, at(4 - go, 0, c), c, at(go, 0, c))

    def third(t):
        for c in range(2):
            arrive(t, at(2, 0, c), c)
            spread(t, at(2, 0, c), c)

    def fourth(t):
        for u in (0, 1, 3, 2):
            for c in range(2):
                go = 1 if u % 2 == 0 else 3
                arrive(t, at(u, 4 - go, c), c)
                send(t, at(u, 4 - go, c), c, at(0, go, c))

    def fifth(t):
        for u in range(4):
            for c in range(2):
                go = 1 if u % 2 == 0 else 3
                arrive(t, at(u, go, c), c)
                arrive(t, at(u, 2, c), c)

    def turn(i):
        @pl.when(i + 2 < TILES)
        def _():
            first(i + 2)

        @pl.when(i + 1 < TILES)
        def _():
            second(i + 1)

        @pl.when(i >= 0)
        def _():
            fourth(i)

        @pl.when(i + 1 < TILES)
        def _():
            third(i + 1)

    first(0)

    def plane_in(d, _):
        p = me ^ d
        wait(ints.at[pl.ds(ints_row(z, p), 32)], plane_recv.at[p])
        line_copy(z, p, up)
        line_copy(z, p, down)
        return _

    lax.fori_loop(1, 16, plane_in, None)

    def pair_part(zs, yhi, core):
        return ints.at[pl.ds(pl.multiple_of(((zs * 2 + yhi) * 2 + core) * 256, 256), 256)]

    def pair_out(zs):
        for yhi in range(2):
            pltpu.make_async_remote_copy(
                pair_part(zs, yhi, k), pair_part(zs, yhi, k), pair_send, pair_recv.at[zs * 2 + yhi],
                device_id=device(x, y, z, 1 - k), device_id_type=MESH,
            ).start()

    pair_out(z)

    def relay(p):
        src, to = (z + 3 + 2 * (p % 2)) % 4, (z + 1 + 2 * (p % 2)) % 4
        line_wait(src, p)
        line_copy(src, p, to)

    def opening(step, _):
        turn(step - 1)

        @pl.when((step == 1) | (step == 2))
        def _():
            def one(j, _):
                relay(me ^ ((step - 1) * 8 + j))
                return _

            lax.fori_loop(0, 8, one, None)

        return _

    lax.fori_loop(0, 4, opening, None)

    def rest(p, _):
        line_wait((z + 1 + 2 * (p % 2)) % 4, p)
        return _

    lax.fori_loop(0, 16, rest, None)
    pair_out(up)
    pair_out(down)

    def last(p, _):
        line_wait(far, p)
        return _

    lax.fori_loop(0, 16, last, None)
    pair_out(far)
    for zs in range(4):
        for yhi in range(2):
            wait(pair_part(zs, yhi, 1 - k), pair_recv.at[zs * 2 + yhi])

    def multiply(t):
        def one(n, _):
            to = (z + 2 + 3 * n) % 4
            total = jnp.dot(
                amp[pl.ds(pl.multiple_of(t * 2 * T, 2 * T), 2 * T), :],
                ints[:, pl.ds(pl.multiple_of(to * 256, 256), 256)],
                preferred_element_type=jnp.float32,
            )
            for c in range(2):
                for yhi in range(2):
                    part = total[yhi * T : (yhi + 1) * T, c * 128 : (c + 1) * 128]
                    top = jnp.max(jnp.abs(part), axis=0, keepdims=True)
                    scale = TOP / jnp.maximum(top * LIFT, 1e-28)
                    code = jnp.round((part * LIFT) * scale)
                    codes[t, to * 2 + c, yhi] = code.astype(jnp.int32).astype(jnp.int16)
                    tops[to * 2 + c, pl.ds(yhi * 8 + t, 1), :] = top
                src = codes.at[t, to * 2 + c]
                dst = q_ref.at[z, :, k * TILES + t]
                here = (to == z) & (k == c)

                @pl.when(here)
                def _():
                    pltpu.make_async_copy(src, dst, out_recv.at[z * 2 + k]).start()

                @pl.when(jnp.logical_not(here))
                def _():
                    pltpu.make_async_remote_copy(
                        src, dst, out_send.at[t], out_recv.at[z * 2 + k],
                        device_id=device(x, y, to, c), device_id_type=MESH,
                    ).start()

            return _

        lax.fori_loop(0, 4, one, None)

    tops[...] = jnp.zeros_like(tops)

    def closing(t, _):
        fifth(t)
        multiply(t)

        @pl.when((t >= 1) & (t <= 2))
        def _():
            turn(t + 2)

        return _

    lax.fori_loop(0, TILES, closing, None)

    for d in range(4):
        for c in range(2):
            to = (z + d) % 4
            src, dst = tops.at[to * 2 + c], m_ref.at[z, k]
            if d:
                pltpu.make_async_remote_copy(
                    src, dst, top_send.at[d * 2 + c], top_recv.at[z * 2 + k],
                    device_id=device(x, y, to, c), device_id_type=MESH,
                ).start()
    other = pltpu.make_async_remote_copy(
        tops.at[z * 2 + 1 - k], m_ref.at[z, k], top_send.at[0], top_recv.at[z * 2 + k],
        device_id=device(x, y, z, 1 - k), device_id_type=MESH,
    )
    other.start()
    pltpu.make_async_copy(tops.at[z * 2 + k], m_ref.at[z, k], top_recv.at[z * 2 + k]).start()

    wait(ipack.at[0:15], plane_send)
    wait(ints.at[0 : 48 * 32], line_send)
    wait(ints.at[0 : 8 * 256], pair_send)
    for t in range(TILES):
        wait(amp.at[0 : 30 * T * 256 // 4096], amp_send.at[t])
        wait(codes.at[t, 0:7], out_send.at[t])
    wait(tops.at[0], top_send.at[0])
    for d in range(1, 4):
        for c in range(2):
            wait(tops.at[0], top_send.at[d * 2 + c])
    for zs in range(4):
        for c in range(2):
            wait(q_ref.at[zs, :, c * TILES : (c + 1) * TILES], out_recv.at[zs * 2 + c])
            wait(m_ref.at[zs, c], top_recv.at[zs * 2 + c])


def decode_kernel(block_rows, q_ref, m_ref, o_ref):
    for r in range(4):
        for n in range(2 * TILES):
            rows = min(T, block_rows - n * T)
            if rows <= 0:
                continue
            code = q_ref[r, n * T : (n + 1) * T, :].astype(jnp.int32).astype(jnp.float32)
            at = (r % 2) * 8 + n % TILES
            top = m_ref[r // 2, n // TILES, at : at + 1, :]
            value = (code * (1.0 / TOP)) * top
            o_ref[r * block_rows + n * T : r * block_rows + n * T + rows, :] = value[0:rows]


def shards(amplitudes, integrals, storage_slot):
    dma = pltpu.SemaphoreType.DMA
    bf16 = jnp.bfloat16
    vmem = pl.BlockSpec(memory_space=pltpu.VMEM)
    hbm = pl.BlockSpec(memory_space=pl.ANY)
    codes, tops = pl.pallas_call(
        ladder_kernel,
        out_shape=(
            jax.ShapeDtypeStruct((4, 2, 2 * TILES, T, 128), jnp.int16),
            jax.ShapeDtypeStruct((4, 2, 16, 128), jnp.float32),
        ),
        in_specs=[vmem] * 3,
        out_specs=(hbm, hbm),
        scratch_shapes=[
            pltpu.VMEM((2 * HALF, 256), bf16),
            pltpu.VMEM((HALF, 512), bf16),
            pltpu.VMEM((512, 512), bf16),
            pltpu.VMEM((8, 512), jnp.int32),
            pltpu.VMEM((16, 32, 1024), bf16),
            pltpu.VMEM((2 * HALF, 4096), bf16),
            pltpu.VMEM((4096, 1024), bf16),
            pltpu.VMEM((TILES, 8, 2, T, 128), jnp.int16),
            pltpu.VMEM((8, 16, 128), jnp.float32),
            dma, dma, dma, dma, dma,
            dma, dma((16,)), dma, dma((64,)), dma, dma((8,)),
            dma((TILES,)), dma((TILES * 32,)), dma((TILES,)), dma((8,)), dma((8,)), dma((8,)),
        ],
        compiler_params=pltpu.CompilerParams(
            collective_id=0, has_side_effects=True, vmem_limit_bytes=56 * 2**20
        ),
    )(amplitudes, integrals, jnp.broadcast_to(storage_slot[None, :], (8, 512)))
    rows = amplitudes.shape[0]
    return pl.pallas_call(
        functools.partial(decode_kernel, rows),
        grid=(2,),
        out_shape=jax.ShapeDtypeStruct((8 * rows, 128), jnp.float32),
        in_specs=[
            pl.BlockSpec((4, 2 * HALF, 128), lambda g: (g, 0, 0)),
            pl.BlockSpec((2, 2, 16, 128), lambda g: (g, 0, 0, 0)),
        ],
        out_specs=pl.BlockSpec((4 * rows, 128), lambda g: (g, 0)),
        compiler_params=pltpu.CompilerParams(vmem_limit_bytes=32 * 2**20),
    )(codes.reshape(8, 2 * HALF, 128), tops)


def solution(mesh):
    in_specs = (P("row", "col"), P(("row", "col"), None), P("row"))
    out_specs = P(None, ("col", "row"))
    return jax.shard_map(shards, mesh=mesh, in_specs=in_specs, out_specs=out_specs, check_vma=False)
```

time: 307 us -> 110 us (0.36)
  waiting for transfers between devices: 192 us -> 0 us
  Pallas kernels: 0 us -> 105 us
  blocking collectives: 65.9 us -> 0 us
  matrix products: 15.5 us -> 0 us
  between operations: 13.5 us -> 0.02 us
  local copies, waits for them, and re-layouts: 11.2 us -> 3.86 us
  starting transfers between devices: 6.91 us -> 0 us
    all_gather x2 -> x0, waiting for transfers between devices: 176 us -> none  [the longest x1 107 us: shards(): int_whole = lax.all_gather(ordered, 'row', axis=0, tiled=True)]
    pallas_call x0 -> x2, Pallas kernels: none -> 105 us  [the longest x1 102 us: shards(): pl.pallas_call(ladder_kernel, out_shape=(jax.ShapeDtypeStruct((4, 2, 2 *...]
    all_to_all x1 -> x0, blocking collectives: 65.9 us -> none  [shards(): lax.all_to_all(ladder, 'row', split_axis=1, concat_axis=0, tiled=True)]
    dot_general x1 -> x0, matrix products: 15.5 us -> none  [shards(): jnp.dot(lax.all_gather(amplitudes, 'col', axis=1, tiled=True), int_whole,...]
    all_to_all x1 -> x0, waiting for transfers between devices: 15 us -> none  [shards(): lax.all_to_all(integrals, 'col', split_axis=1, concat_axis=0, tiled=True)]
    all_to_all x4 -> x0, local copies, waits for them, and re-layouts: 7.86 us -> none  [the longest x3 5.58 us: shards(): lax.all_to_all(ladder, 'row', split_axis=1, concat_axis=0, tiled=True)]
    all_to_all x1 -> x0, starting transfers between devices: 6.83 us -> none  [shards(): lax.all_to_all(integrals, 'col', split_axis=1, concat_axis=0, tiled=True)]
  transfers between devices with their start and end apart: 3 -> 0, of which waited for: 3 -> 0; matrix products, arithmetic and copies ran while one was open for 0% -> 0% of each run, Pallas kernels for 0% -> 0%
where the time goes in v1:
time: 110 us; the launch traced here: 109 us
  Pallas kernels  105 us (95%)
  local copies, waits for them, and re-layouts  3.86 us (4%)
    pallas_call x1, Pallas kernels, shards(): pl.pallas_call(ladder_kernel, out_shape=(jax.ShapeDtypeStruct((4, 2, 2 *...  102 us
    pallas_call x1, Pallas kernels, shards(): pl.pallas_call(functools.partial(decode_kernel, rows), grid=(2,), out_sha...  2.65 us
    unnamed x4, local copies, waits for them, and re-layouts  2.57 us

profile of v1, /device:TPU:1, one launch (start us, length us, event | category | flops | bytes accessed | tf_op | source)
XLA Modules:
  0.0 108.9 jit_solution(4673642495098489320)
XLA Ops:
  0.0 1.3 %broadcast_in_dim.2.slot_ref = s32[8,512]{1,0:T(8,128)} broadcast(s32[512]{0:T(512)} %param.5), dimensions={1} | broadcast | bytes 18432 | tf_op jit(solution)/shard_map/broadcast_in_dim | solution.py:429
  1.3 102.4 %shard_map.37 = (s16[4,2,10,128,128]{4,3,2,1,0:T(8,128)(2,1)}, f32[4,2,16,128]{3,2,1,0:T(8,128)}) custom-call(bf16[1250,256]{1,0:T(8,128)(2,1)} %a_ref.1, bf16[32,16384]{1,0:T(8,128)(2,1)} %i_ref.1, s32[8,512]{1,0:T(8,128)} %broadcast_in_dim.2.slot_ref), custom_call_target="tpu_custom_call" | custom-call | tf_op jit(solution)/shard_map/pallas_call | solution.py:404
  103.7 0.0 copy-start
  103.7 1.7 %copy-done = s16[4,2,10,128,128]{4,3,2,1,0:T(8,128)(2,1)S(1)} copy-done((s16[4,2,10,128,128]{4,3,2,1,0:T(8,128)(2,1)S(1)}, s16[4,2,10,128,128]{4,3,2,1,0:T(8,128)(2,1)}, u32[]{:S(2)}) %copy-start) | copy-done | bytes 2621464
  105.4 0.0 copy-start.1
  105.4 0.8 copy-done.1
  106.2 2.6 %shard_map.38 = f32[10000,128]{1,0:T(8,128)} custom-call(s16[8,1280,128]{2,1,0:T(8,128)(2,1)S(1)} %bitcast.1, f32[4,2,16,128]{3,2,1,0:T(8,128)S(1)} %copy-done.1), custom_call_target="tpu_custom_call" | custom-call | tf_op jit(solution)/shard_map/pallas_call | solution.py:431
Async XLA Ops:
  103.7 1.7 %copy-start = (s16[4,2,10,128,128]{4,3,2,1,0:T(8,128)(2,1)S(1)}, s16[4,2,10,128,128]{4,3,2,1,0:T(8,128)(2,1)}, u32[]{:S(2)}) copy-start(s16[4,2,10,128,128]{4,3,2,1,0:T(8,128)(2,1)} %get-tuple-element.7) | copy-start | bytes 7864324
  105.4 0.8 copy-start.1

commit v2 on v1

--- a/solution.py
+++ b/solution.py
@@ -13,6 +13,10 @@
 HALF = T * TILES
 LIFT = 2.0**40
 TOP = 32767.0
+STEPS = (
+    (1, 0), (3, 0), (0, 1), (0, 3), (1, 1), (3, 3), (1, 3), (3, 1),
+    (2, 0), (0, 2), (2, 1), (2, 3), (1, 2), (3, 2), (2, 2),
+)
 
 
 def device(x, y, z, k):
@@ -110,16 +114,15 @@
 
     up, down, far = (z + 1) % 4, (z + 3) % 4, (z + 2) % 4
 
-    def plane_out(d, _):
-        p = me ^ d
-        px, py = chip_of(p)
-        pltpu.make_async_remote_copy(
-            ipack.at[p], ints.at[mine], plane_send, plane_recv.at[me],
-            device_id=device(px, py, z, k), device_id_type=MESH,
-        ).start()
-        return _
-
-    lax.fori_loop(1, 16, plane_out, None)
+    def plane_out(steps):
+        for dx, dy in steps:
+            px, py = (x + dx) % 4, (y + dy) % 4
+            pltpu.make_async_remote_copy(
+                ipack.at[place(px, py)], ints.at[mine], plane_send, plane_recv.at[me],
+                device_id=device(px, py, z, k), device_id_type=MESH,
+            ).start()
+
+    plane_out(STEPS[:8])
     line_copy(z, me, up)
     line_copy(z, me, down)
 
@@ -184,9 +187,6 @@
     def arrive(t, src, c):
         wait(piece(t, *src, c), amp_sem(t, *src, c))
 
-    def when(cond):
-        return pl.when(cond) if not isinstance(cond, bool) else (lambda f: f() if cond else None)
-
     def first(t):
         for c in range(2):
             for s in (1, 3):
@@ -224,33 +224,21 @@
                 arrive(t, at(u, go, c), c)
                 arrive(t, at(u, 2, c), c)
 
-    def turn(i):
-        @pl.when(i + 2 < TILES)
-        def _():
-            first(i + 2)
-
-        @pl.when(i + 1 < TILES)
-        def _():
-            second(i + 1)
-
-        @pl.when(i >= 0)
-        def _():
-            fourth(i)
-
-        @pl.when(i + 1 < TILES)
-        def _():
-            third(i + 1)
-
+    sources = [me] + [place((x + 4 - dx) % 4, (y + 4 - dy) % 4) for dx, dy in STEPS]
+
+    def plane_in(parts):
+        for p in parts:
+            wait(ints.at[pl.ds(ints_row(z, p), 32)], plane_recv.at[p])
+            line_copy(z, p, up)
+            line_copy(z, p, down)
+
+    plane_out(STEPS[8:])
     first(0)
-
-    def plane_in(d, _):
-        p = me ^ d
-        wait(ints.at[pl.ds(ints_row(z, p), 32)], plane_recv.at[p])
-        line_copy(z, p, up)
-        line_copy(z, p, down)
-        return _
-
-    lax.fori_loop(1, 16, plane_in, None)
+    first(1)
+    plane_in(sources[1:12])
+    second(0)
+    plane_in(sources[12:])
+    third(0)
 
     def pair_part(zs, yhi, core):
         return ints.at[pl.ds(pl.multiple_of(((zs * 2 + yhi) * 2 + core) * 256, 256), 256)]
@@ -269,20 +257,21 @@
         line_wait(src, p)
         line_copy(src, p, to)
 
-    def opening(step, _):
-        turn(step - 1)
-
-        @pl.when((step == 1) | (step == 2))
-        def _():
-            def one(j, _):
-                relay(me ^ ((step - 1) * 8 + j))
-                return _
-
-            lax.fori_loop(0, 8, one, None)
-
-        return _
-
-    lax.fori_loop(0, 4, opening, None)
+    def relays(parts):
+        for p in parts:
+            relay(p)
+
+    relays(sources[0:4])
+    first(2)
+    second(1)
+    fourth(0)
+    third(1)
+    relays(sources[4:10])
+    first(3)
+    second(2)
+    relays(sources[10:])
+    fourth(1)
+    third(2)
 
     def rest(p, _):
         line_wait((z + 1 + 2 * (p % 2)) % 4, p)
@@ -291,6 +280,8 @@
     lax.fori_loop(0, 16, rest, None)
     pair_out(up)
     pair_out(down)
+    first(4)
+    second(3)
 
     def last(p, _):
         line_wait(far, p)
@@ -343,9 +334,20 @@
         fifth(t)
         multiply(t)
 
-        @pl.when((t >= 1) & (t <= 2))
+        @pl.when(t == 0)
         def _():
-            turn(t + 2)
+            fourth(2)
+            third(3)
+
+        @pl.when(t == 1)
+        def _():
+            second(4)
+            fourth(3)
+            third(4)
+
+        @pl.when(t == 2)
+        def _():
+            fourth(4)
 
         return _
 
@@ -413,7 +415,7 @@
             pltpu.VMEM((2 * HALF, 256), bf16),
             pltpu.VMEM((HALF, 512), bf16),
             pltpu.VMEM((512, 512), bf16),
-            pltpu.VMEM((8, 512), jnp.int32),
+            pltpu.VMEM((1, 512), jnp.int32),
             pltpu.VMEM((16, 32, 1024), bf16),
             pltpu.VMEM((2 * HALF, 4096), bf16),
             pltpu.VMEM((4096, 1024), bf16),
@@ -426,7 +428,7 @@
         compiler_params=pltpu.CompilerParams(
             collective_id=0, has_side_effects=True, vmem_limit_bytes=56 * 2**20
         ),
-    )(amplitudes, integrals, jnp.broadcast_to(storage_slot[None, :], (8, 512)))
+    )(amplitudes, integrals, storage_slot.reshape(1, 512))
     rows = amplitudes.shape[0]
     return pl.pallas_call(
         functools.partial(decode_kernel, rows),
@@ -437,7 +439,7 @@
             pl.BlockSpec((2, 2, 16, 128), lambda g: (g, 0, 0, 0)),
         ],
         out_specs=pl.BlockSpec((4 * rows, 128), lambda g: (g, 0)),
-        compiler_params=pltpu.CompilerParams(vmem_limit_bytes=32 * 2**20),
+        compiler_params=pltpu.CompilerParams(vmem_limit_bytes=60 * 2**20),
     )(codes.reshape(8, 2 * HALF, 128), tops)
 
 

time: 110 us -> 101 us (0.918)
  Pallas kernels: 105 us -> 101 us
  local copies, waits for them, and re-layouts: 3.86 us -> 0 us
    pallas_call x1, Pallas kernels: 102 us -> 96.6 us  [shards(): pl.pallas_call(ladder_kernel, out_shape=(jax.ShapeDtypeStruct((4, 2, 2 *...]
    unnamed x4 -> x0, local copies, waits for them, and re-layouts: 2.57 us -> none
    pallas_call x1, Pallas kernels: 2.65 us -> 3.98 us  [shards(): pl.pallas_call(functools.partial(decode_kernel, rows), grid=(2,), out_sha...]
    broadcast_in_dim x1 -> x0, local copies, waits for them, and re-layouts: 1.29 us -> none  [shards(): jnp.broadcast_to(storage_slot[None, :], (8, 512))]
where the time goes in v2:
time: 101 us
  Pallas kernels  101 us (100%)
    pallas_call x1, Pallas kernels, shards(): pl.pallas_call(ladder_kernel, out_shape=(jax.ShapeDtypeStruct((4, 2, 2 *...  96.6 us
    pallas_call x1, Pallas kernels, shards(): pl.pallas_call(functools.partial(decode_kernel, rows), grid=(2,), out_sha...  3.98 us

profile of v2, /device:TPU:1, one launch (start us, length us, event | category | flops | bytes accessed | tf_op | source)
XLA Modules:
  0.0 100.6 jit_solution(11662334022585176379)
XLA Ops:
  0.0 96.6 %shard_map.37 = (s16[4,2,10,128,128]{4,3,2,1,0:T(8,128)(2,1)}, f32[4,2,16,128]{3,2,1,0:T(8,128)}) custom-call(bf16[1250,256]{1,0:T(8,128)(2,1)} %a_ref.1, bf16[32,16384]{1,0:T(8,128)(2,1)} %i_ref.1, s32[1,512]{1,0:T(1,128)} %bitcast.3), custom_call_target="tpu_custom_call" | custom-call | tf_op jit(solution)/shard_map/pallas_call | solution.py:406
  96.6 4.0 %shard_map.38 = f32[10000,128]{1,0:T(8,128)} custom-call(s16[8,1280,128]{2,1,0:T(8,128)(2,1)} %bitcast.2, f32[4,2,16,128]{3,2,1,0:T(8,128)} %get-tuple-element.8.m_ref), custom_call_target="tpu_custom_call" | custom-call | tf_op jit(solution)/shard_map/pallas_call | solution.py:433

commit v3 on v2

v3 whole, which is shorter than its diff:
```python
import functools

import jax
import jax.numpy as jnp
from jax import lax
from jax.experimental import pallas as pl
from jax.experimental.pallas import tpu as pltpu
from jax.sharding import PartitionSpec as P

MESH = pl.DeviceIdType.MESH
SIZES = (160, 160, 128, 128, 64)
TILES = len(SIZES)
STARTS = tuple(sum(SIZES[:t]) for t in range(TILES))
HALF = sum(SIZES)
LIFT = 2.0**40
TOP = 32767.0
STEPS = (
    (1, 0), (3, 0), (0, 1), (0, 3), (1, 1), (3, 3), (1, 3), (3, 1),
    (2, 0), (0, 2), (2, 1), (2, 3), (1, 2), (3, 2), (2, 2),
)


def device(x, y, z, k):
    return (z * 2 + (y >> 1), x * 4 + (y & 1) * 2 + k)


def wait(ref, sem):
    pltpu.make_async_copy(ref, ref, sem).wait()


def ladder_kernel(
    a_ref, i_ref, slot_ref, q_ref, m_ref,
    apad, lhs, onehot, slots, ipack, amp, ints, codes, tops,
    slot_send, slot_recv, half_send, half_recv,
    plane_send, plane_recv, line_send, line_recv, pair_send, pair_recv,
    amp_send, amp_recv, out_send, out_recv, top_send, top_recv,
):
    row, col = lax.axis_index("row"), lax.axis_index("col")
    x, y, z, k = col >> 2, (row & 1) * 2 + ((col >> 1) & 1), row >> 1, col & 1
    yhi_here = row & 1
    xs, ys = [(x + d) & 3 for d in range(4)], [(y + d) & 3 for d in range(4)]
    me = yhi_here * 8 + (col >> 1)

    def chip_of(p):
        return (p & 7) >> 1, (p >> 3) * 2 + (p & 1)

    def place(px, py):
        return (py >> 1) * 8 + px * 2 + (py & 1)

    barrier = pltpu.get_barrier_semaphore()

    def greet(d):
        pl.semaphore_signal(barrier, inc=1, device_id=d, device_id_type=MESH)

    for dx, dy in reversed(STEPS):
        greet(device(xs[dx], ys[dy], z, k))
    for d in range(1, 4):
        for c in range(2):
            greet(device(x, y, (z + d) & 3, c))
    greet(device(x, y, z, 1 - k))
    turned = (y & 1) * 2 + (y >> 1)
    for d in range(1, 4):
        greet(device(x, turned, (z + d) & 3, k))

    def pack(p, _):
        px, py = chip_of(p)
        base = (px * 2 + (py & 1)) * 16 + (py >> 1)
        for zz in range(4):
            for c in range(2):
                at = pl.multiple_of((base + c * 8 + zz * 2) * 128, 128)
                ipack[p, :, (zz * 2 + c) * 128 : (zz * 2 + c + 1) * 128] = i_ref[:, pl.ds(at, 128)]
        return _

    lax.fori_loop(0, 16, pack, None)
    rows = a_ref.shape[0]
    low = rows // 16 * 16
    apad[low:, :] = jnp.zeros((2 * HALF - low, 256), jnp.bfloat16)
    apad[0:rows, :] = a_ref[...]

    def ints_row(zs, p):
        return pl.multiple_of(((zs * 2 + (p >> 3)) * 2 + k) * 256 + (p & 7) * 32, 32)

    mine = pl.ds(ints_row(z, me), 32)
    ints[mine, :] = ipack[me]

    pl.semaphore_wait(barrier, 25)

    def slot_copy(d):
        return pltpu.make_async_remote_copy(
            slot_ref, slots, slot_send.at[d], slot_recv, device_id=device(x, turned, (z + d) & 3, k), device_id_type=MESH
        )

    holds, fixed = z == x, turned == y

    @pl.when(holds)
    def _():
        for d in range(1, 4):
            slot_copy(d).start()

    @pl.when(holds & jnp.logical_not(fixed))
    def _():
        slot_copy(0).start()

    half_copy = pltpu.make_async_remote_copy(
        apad.at[pl.ds(pl.multiple_of((1 - k) * HALF, 32), HALF)],
        lhs.at[:, pl.ds(pl.multiple_of(k * 256, 256), 256)],
        half_send, half_recv, device_id=device(x, y, z, 1 - k), device_id_type=MESH,
    )
    half_copy.start()

    def line_copy(zs, p, to):
        part = ints.at[pl.ds(ints_row(zs, p), 32)]
        pltpu.make_async_remote_copy(
            part, part, line_send, line_recv.at[zs * 16 + p], device_id=device(x, y, to, k), device_id_type=MESH
        ).start()

    def line_wait(zs, p):
        wait(ints.at[pl.ds(ints_row(zs, p), 32)], line_recv.at[zs * 16 + p])

    up, down, far = (z + 1) & 3, (z + 3) & 3, (z + 2) & 3

    def plane_out(steps):
        for dx, dy in steps:
            px, py = xs[dx], ys[dy]
            pltpu.make_async_remote_copy(
                ipack.at[place(px, py)], ints.at[mine], plane_send, plane_recv.at[me],
                device_id=device(px, py, z, k), device_id_type=MESH,
            ).start()

    plane_out(STEPS[:8])
    line_copy(z, me, up)
    line_copy(z, me, down)

    def amp_rows(t, yhi):
        return pl.ds(pl.multiple_of(STARTS[t] * 2 + yhi * SIZES[t], 32), SIZES[t])

    def piece(t, px, py, c):
        return amp.at[
            amp_rows(t, py >> 1),
            pl.ds(pl.multiple_of(px * 1024 + (py & 1) * 512 + c * 256, 256), 256),
        ]

    def at(u, v, c):
        fx, fy = (u, v) if c == 0 else (v, u)
        return xs[fx], ys[fy]

    def amp_sem(t, px, py, c):
        return amp_recv.at[(t * 16 + place(px, py)) * 2 + c]

    def send(t, src, c, to):
        part = piece(t, *src, c)
        pltpu.make_async_remote_copy(
            part, part, amp_send.at[t], amp_sem(t, *src, c), device_id=device(*to, z, k), device_id_type=MESH
        ).start()

    def arrive(t, src, c):
        wait(piece(t, *src, c), amp_sem(t, *src, c))

    def order(t):
        rows = slice(STARTS[t], STARTS[t] + SIZES[t])
        part = jnp.dot(lhs[rows, :], onehot[...], preferred_element_type=jnp.float32)
        amp[amp_rows(t, yhi_here), pl.ds(pl.multiple_of(block * 512, 512), 512)] = part.astype(jnp.bfloat16)

    def first(t):
        for c in range(2):
            for s in (1, 3):
                send(t, at(0, 0, c), c, at(s, 0, c))

    def spread(t, src, c):
        for s in (1, 3):
            send(t, src, c, at(0, s, c))

    def second(t):
        for c in range(2):
            spread(t, at(0, 0, c), c)
            for s in (1, 3):
                arrive(t, at(s, 0, c), c)
                spread(t, at(s, 0, c), c)
            go = 1 + 2 * ((t + c) % 2)
            send(t, at(4 - go, 0, c), c, at(go, 0, c))

    def third(t):
        for c in range(2):
            arrive(t, at(2, 0, c), c)
            spread(t, at(2, 0, c), c)

    def fourth(t):
        for u in (0, 1, 3, 2):
            for c in range(2):
                go = 1 if u % 2 == 0 else 3
                arrive(t, at(u, 4 - go, c), c)
                send(t, at(u, 4 - go, c), c, at(0, go, c))

    def fifth(t):
        for u in range(4):
            for c in range(2):
                go = 1 if u % 2 == 0 else 3
                arrive(t, at(u, go, c), c)
                arrive(t, at(u, 2, c), c)

    def pair_part(zs, yhi, core):
        return ints.at[pl.ds(pl.multiple_of(((zs * 2 + yhi) * 2 + core) * 256, 256), 256)]

    def pair_out(zs):
        for yhi in range(2):
            pltpu.make_async_remote_copy(
                pair_part(zs, yhi, k), pair_part(zs, yhi, k), pair_send, pair_recv.at[zs * 2 + yhi],
                device_id=device(x, y, z, 1 - k), device_id_type=MESH,
            ).start()

    def pair_in(zs):
        for yhi in range(2):
            wait(pair_part(zs, yhi, 1 - k), pair_recv.at[zs * 2 + yhi])

    sources = [me] + [place(xs[-dx % 4], ys[-dy % 4]) for dx, dy in STEPS]

    def plane_in(parts):
        for p in parts:
            wait(ints.at[pl.ds(ints_row(z, p), 32)], plane_recv.at[p])
            line_copy(z, p, up)
            line_copy(z, p, down)

    lhs[:, pl.ds(pl.multiple_of(k * 256, 256), 256)] = apad[pl.ds(pl.multiple_of(k * HALF, 32), HALF), :]

    @pl.when(holds & fixed)
    def _():
        slots[...] = slot_ref[...]

    @pl.when(jnp.logical_not(holds & fixed))
    def _():
        wait(slots, slot_recv)

    block = col >> 1
    for q in range(4):
        want = jnp.broadcast_to(slots[q : q + 1, :] - block * 512, (128, 128)).T
        for s in range(4):
            place_of = lax.broadcasted_iota(jnp.int32, (128, 128), 1) + s * 128
            stored = ((place_of & 255) >> 5) * 64 + (place_of >> 8) * 32 + (place_of & 31)
            hit = jnp.where(want == stored, 1.0, 0.0).astype(jnp.bfloat16)
            onehot[q * 128 : (q + 1) * 128, s * 128 : (s + 1) * 128] = hit
    half_copy.wait()
    order(0)
    first(0)
    plane_out(STEPS[8:])
    order(1)
    first(1)
    plane_in(sources[1:8])
    for t in range(2, TILES):
        order(t)
    plane_in(sources[8:12])
    second(0)
    plane_in(sources[12:])
    pair_out(z)
    third(0)

    def relay(p):
        src, to = (z + 3 + 2 * (p & 1)) & 3, (z + 1 + 2 * (p & 1)) & 3
        line_wait(src, p)
        line_copy(src, p, to)

    def relays(parts):
        for p in parts:
            relay(p)

    relays(sources[0:4])
    first(2)
    second(1)
    fourth(0)
    third(1)
    relays(sources[4:10])
    first(3)
    second(2)
    relays(sources[10:])
    fourth(1)
    third(2)

    def rest(p, _):
        line_wait((z + 1 + 2 * (p & 1)) & 3, p)
        return _

    lax.fori_loop(0, 16, rest, None)
    pair_out(up)
    pair_out(down)
    first(4)
    second(3)

    def last(p, _):
        line_wait(far, p)
        return _

    lax.fori_loop(0, 16, last, None)
    pair_out(far)
    for zs in range(4):
        pair_in(zs)

    def multiply(t):
        size, start = SIZES[t], STARTS[t]

        def one(n, _):
            to = (z + 2 + 3 * n) & 3
            total = jnp.dot(
                amp[2 * start : 2 * (start + size), :],
                ints[:, pl.ds(pl.multiple_of(to * 256, 256), 256)],
                preferred_element_type=jnp.float32,
            )
            for c in range(2):
                for yhi in range(2):
                    part = total[yhi * size : (yhi + 1) * size, c * 128 : (c + 1) * 128]
                    top = jnp.max(jnp.abs(part), axis=0, keepdims=True)
                    scale = TOP / jnp.maximum(top * LIFT, 1e-28)
                    code = jnp.round((part * LIFT) * scale)
                    codes[to * 2 + c, yhi, start : start + size, :] = code.astype(jnp.int32).astype(jnp.int16)
                    tops[to * 2 + c, yhi * 8 + t : yhi * 8 + t + 1, :] = top
                src = codes.at[to * 2 + c, :, pl.ds(start, size)]
                dst = q_ref.at[z, :, pl.ds(pl.multiple_of(k * HALF + start, 32), size)]
                here = (to == z) & (k == c)

                @pl.when(here)
                def _():
                    pltpu.make_async_copy(src, dst, out_recv.at[z * 2 + k]).start()

                @pl.when(jnp.logical_not(here))
                def _():
                    pltpu.make_async_remote_copy(
                        src, dst, out_send.at[t], out_recv.at[z * 2 + k],
                        device_id=device(x, y, to, c), device_id_type=MESH,
                    ).start()

            return _

        lax.fori_loop(0, 4, one, None)

    tops[...] = jnp.zeros_like(tops)

    for t in range(TILES):
        fifth(t)
        multiply(t)
        if t + 4 < TILES and t > 0:
            first(t + 4)
        if t + 3 < TILES and t > 0:
            second(t + 3)
        if t + 2 < TILES:
            fourth(t + 2)
        if t + 3 < TILES:
            third(t + 3)

    for d in range(4):
        for c in range(2):
            to = (z + d) & 3
            src, dst = tops.at[to * 2 + c], m_ref.at[z, k]
            if d:
                pltpu.make_async_remote_copy(
                    src, dst, top_send.at[d * 2 + c], top_recv.at[z * 2 + k],
                    device_id=device(x, y, to, c), device_id_type=MESH,
                ).start()
    other = pltpu.make_async_remote_copy(
        tops.at[z * 2 + 1 - k], m_ref.at[z, k], top_send.at[0], top_recv.at[z * 2 + k],
        device_id=device(x, y, z, 1 - k), device_id_type=MESH,
    )
    other.start()
    pltpu.make_async_copy(tops.at[z * 2 + k], m_ref.at[z, k], top_recv.at[z * 2 + k]).start()

    wait(ipack.at[0:15], plane_send)
    wait(ints.at[0 : 48 * 32], line_send)
    wait(ints.at[0 : 8 * 256], pair_send)
    for t in range(TILES):
        wait(ints.at[0 : 30 * SIZES[t] // 4], amp_send.at[t])
        wait(codes.at[0:7, :, pl.ds(STARTS[t], SIZES[t])], out_send.at[t])

    @pl.when(holds)
    def _():
        for d in range(1, 4):
            slot_copy(d).wait_send()

    @pl.when(holds & jnp.logical_not(fixed))
    def _():
        slot_copy(0).wait_send()

    wait(tops.at[0], top_send.at[0])
    for d in range(1, 4):
        for c in range(2):
            wait(tops.at[0], top_send.at[d * 2 + c])
    for zs in range(4):
        for c in range(2):
            wait(q_ref.at[zs, :, c * HALF : (c + 1) * HALF], out_recv.at[zs * 2 + c])
            wait(m_ref.at[zs, c], top_recv.at[zs * 2 + c])


def decode_kernel(block_rows, q_ref, m_ref, o_ref, codes, values, in_sem, out_sem):
    ins = [pltpu.make_async_copy(q_ref.at[r], codes.at[r], in_sem.at[r]) for r in range(8)]
    for copy in ins:
        copy.start()
    outs = []
    for r in range(8):
        ins[r].wait()
        for h in range(2):
            for t in range(TILES):
                at = h * HALF + STARTS[t]
                rows = min(SIZES[t], block_rows - at)
                if rows <= 0:
                    continue
                code = codes[r, at : at + SIZES[t], :].astype(jnp.int32).astype(jnp.float32)
                line = (r % 2) * 8 + t
                value = (code * (1.0 / TOP)) * m_ref[r // 2, h, line : line + 1, :]
                values[r * block_rows + at : r * block_rows + at + rows, :] = value[0:rows]
        low, high = r * block_rows // 8 * 8, (r + 1) * block_rows // 8 * 8
        copy = pltpu.make_async_copy(values.at[low:high], o_ref.at[low:high], out_sem.at[r])
        copy.start()
        outs.append(copy)
    for copy in outs:
        copy.wait()


def shards(amplitudes, integrals, storage_slot):
    dma = pltpu.SemaphoreType.DMA
    bf16 = jnp.bfloat16
    vmem = pl.BlockSpec(memory_space=pltpu.VMEM)
    hbm = pl.BlockSpec(memory_space=pl.ANY)
    codes, tops = pl.pallas_call(
        ladder_kernel,
        out_shape=(
            jax.ShapeDtypeStruct((4, 2, 2 * HALF, 128), jnp.int16),
            jax.ShapeDtypeStruct((4, 2, 16, 128), jnp.float32),
        ),
        in_specs=[vmem] * 3,
        out_specs=(hbm, hbm),
        scratch_shapes=[
            pltpu.VMEM((2 * HALF, 256), bf16),
            pltpu.VMEM((HALF, 512), bf16),
            pltpu.VMEM((512, 512), bf16),
            pltpu.VMEM((4, 128), jnp.int32),
            pltpu.VMEM((16, 32, 1024), bf16),
            pltpu.VMEM((2 * HALF, 4096), bf16),
            pltpu.VMEM((4096, 1024), bf16),
            pltpu.VMEM((8, 2, HALF, 128), jnp.int16),
            pltpu.VMEM((8, 16, 128), jnp.float32),
            dma((4,)), dma, dma, dma,
            dma, dma((16,)), dma, dma((64,)), dma, dma((8,)),
            dma((TILES,)), dma((TILES * 32,)), dma((TILES,)), dma((8,)), dma((8,)), dma((8,)),
        ],
        compiler_params=pltpu.CompilerParams(
            collective_id=0, has_side_effects=True, vmem_limit_bytes=56 * 2**20
        ),
    )(amplitudes, integrals, storage_slot.reshape(4, 128))
    rows = amplitudes.shape[0]
    return pl.pallas_call(
        functools.partial(decode_kernel, rows),
        out_shape=jax.ShapeDtypeStruct((8 * rows, 128), jnp.float32),
        in_specs=[hbm, vmem],
        out_specs=hbm,
        scratch_shapes=[
            pltpu.VMEM((8, 2 * HALF, 128), jnp.int16),
            pltpu.VMEM((8 * rows, 128), jnp.float32),
            dma((8,)), dma((8,)),
        ],
        compiler_params=pltpu.CompilerParams(vmem_limit_bytes=60 * 2**20),
    )(codes.reshape(8, 2 * HALF, 128), tops)


def solution(mesh):
    in_specs = (P("row", "col"), P(("row", "col"), None), P("row"))
    out_specs = P(None, ("col", "row"))
    return jax.shard_map(shards, mesh=mesh, in_specs=in_specs, out_specs=out_specs, check_vma=False)
```

time: 101 us -> 99 us (0.980)
  Pallas kernels: 101 us -> 98.8 us
    pallas_call x1, Pallas kernels: 96.6 us -> 94.5 us  [shards(): pl.pallas_call(ladder_kernel, out_shape=(jax.ShapeDtypeStruct((4, 2, 2 *...]
where the time goes in v3:
time: 99 us; the launch traced here: 98.8 us
  Pallas kernels  98.8 us (100%)
    pallas_call x1, Pallas kernels, shards(): pl.pallas_call(ladder_kernel, out_shape=(jax.ShapeDtypeStruct((4, 2, 2 *...  94.5 us
    pallas_call x1, Pallas kernels, shards(): pl.pallas_call(functools.partial(decode_kernel, rows), out_shape=jax.Shap...  4.34 us

profile of v3, /device:TPU:1, one launch (start us, length us, event | category | flops | bytes accessed | tf_op | source)
XLA Modules:
  0.0 98.8 jit_solution(7404323376558034060)
XLA Ops:
  0.0 94.5 %shard_map.37 = (s16[4,2,1280,128]{3,2,1,0:T(8,128)(2,1)}, f32[4,2,16,128]{3,2,1,0:T(8,128)}) custom-call(bf16[1250,256]{1,0:T(8,128)(2,1)} %a_ref.1, bf16[32,16384]{1,0:T(8,128)(2,1)} %i_ref.1, s32[4,128]{1,0:T(4,128)} %bitcast.3), custom_call_target="tpu_custom_call" | custom-call | tf_op jit(solution)/shard_map/pallas_call | solution.py:419
  94.5 4.3 %shard_map.38 = f32[10000,128]{1,0:T(8,128)} custom-call(s16[8,1280,128]{2,1,0:T(8,128)(2,1)} %bitcast.2, f32[4,2,16,128]{3,2,1,0:T(8,128)} %get-tuple-element.8.m_ref), custom_call_target="tpu_custom_call" | custom-call | tf_op jit(solution)/shard_map/pallas_call | solution.py:446

commit v4 on v3

--- a/solution.py
+++ b/solution.py
@@ -8,7 +8,7 @@
 from jax.sharding import PartitionSpec as P
 
 MESH = pl.DeviceIdType.MESH
-SIZES = (160, 160, 128, 128, 64)
+SIZES = (160, 128, 128, 128, 96)
 TILES = len(SIZES)
 STARTS = tuple(sum(SIZES[:t]) for t in range(TILES))
 HALF = sum(SIZES)
@@ -29,8 +29,8 @@
 
 
 def ladder_kernel(
-    a_ref, i_ref, slot_ref, q_ref, m_ref,
-    apad, lhs, onehot, slots, ipack, amp, ints, codes, tops,
+    a_hbm, i_hbm, slot_hbm, q_ref, m_ref,
+    a_ref, i_ref, slot_ref, in_sem, apad, lhs, onehot, slots, ipack, amp, ints, codes, tops,
     slot_send, slot_recv, half_send, half_recv,
     plane_send, plane_recv, line_send, line_recv, pair_send, pair_recv,
     amp_send, amp_recv, out_send, out_recv, top_send, top_recv,
@@ -47,6 +47,13 @@
     def place(px, py):
         return (py >> 1) * 8 + px * 2 + (py & 1)
 
+    loads = [
+        pltpu.make_async_copy(src, dst, in_sem.at[i])
+        for i, (src, dst) in enumerate(((i_hbm, i_ref), (a_hbm, a_ref), (slot_hbm, slot_ref)))
+    ]
+    for load in loads:
+        load.start()
+
     barrier = pltpu.get_barrier_semaphore()
 
     def greet(d):
@@ -71,11 +78,21 @@
                 ipack[p, :, (zz * 2 + c) * 128 : (zz * 2 + c + 1) * 128] = i_ref[:, pl.ds(at, 128)]
         return _
 
+    loads[0].wait()
     lax.fori_loop(0, 16, pack, None)
     rows = a_ref.shape[0]
     low = rows // 16 * 16
+    apad[0:16, :] = jnp.zeros((16, 256), jnp.bfloat16)
     apad[low:, :] = jnp.zeros((2 * HALF - low, 256), jnp.bfloat16)
-    apad[0:rows, :] = a_ref[...]
+    loads[1].wait()
+    for r in range(4):
+
+        @pl.when((row & 3) == r)
+        def _():
+            lead = rows * r % 8
+            apad[lead : lead + rows, :] = a_ref[...]
+
+    loads[2].wait()
 
     def ints_row(zs, p):
         return pl.multiple_of(((zs * 2 + (p >> 3)) * 2 + k) * 256 + (p & 7) * 32, 32)
@@ -239,20 +256,6 @@
             hit = jnp.where(want == stored, 1.0, 0.0).astype(jnp.bfloat16)
             onehot[q * 128 : (q + 1) * 128, s * 128 : (s + 1) * 128] = hit
     half_copy.wait()
-    order(0)
-    first(0)
-    plane_out(STEPS[8:])
-    order(1)
-    first(1)
-    plane_in(sources[1:8])
-    for t in range(2, TILES):
-        order(t)
-    plane_in(sources[8:12])
-    second(0)
-    plane_in(sources[12:])
-    pair_out(z)
-    third(0)
-
     def relay(p):
         src, to = (z + 3 + 2 * (p & 1)) & 3, (z + 1 + 2 * (p & 1)) & 3
         line_wait(src, p)
@@ -262,36 +265,13 @@
         for p in parts:
             relay(p)
 
-    relays(sources[0:4])
-    first(2)
-    second(1)
-    fourth(0)
-    third(1)
-    relays(sources[4:10])
-    first(3)
-    second(2)
-    relays(sources[10:])
-    fourth(1)
-    third(2)
-
     def rest(p, _):
         line_wait((z + 1 + 2 * (p & 1)) & 3, p)
         return _
 
-    lax.fori_loop(0, 16, rest, None)
-    pair_out(up)
-    pair_out(down)
-    first(4)
-    second(3)
-
     def last(p, _):
         line_wait(far, p)
         return _
-
-    lax.fori_loop(0, 16, last, None)
-    pair_out(far)
-    for zs in range(4):
-        pair_in(zs)
 
     def multiply(t):
         size, start = SIZES[t], STARTS[t]
@@ -332,17 +312,55 @@
 
     tops[...] = jnp.zeros_like(tops)
 
-    for t in range(TILES):
-        fifth(t)
-        multiply(t)
-        if t + 4 < TILES and t > 0:
-            first(t + 4)
-        if t + 3 < TILES and t > 0:
-            second(t + 3)
-        if t + 2 < TILES:
-            fourth(t + 2)
-        if t + 3 < TILES:
-            third(t + 3)
+    order(0)
+    first(0)
+    plane_out(STEPS[8:])
+    order(1)
+    first(1)
+    plane_in(sources[1:8])
+    order(2)
+    order(3)
+    order(4)
+    plane_in(sources[8:12])
+    second(0)
+    plane_in(sources[12:16])
+    pair_out(z)
+    third(0)
+    first(2)
+    second(1)
+    relays(sources[0:6])
+    fourth(0)
+    third(1)
+    first(3)
+    second(2)
+    relays(sources[6:16])
+    fourth(1)
+    third(2)
+    lax.fori_loop(0, 16, rest, None)
+    pair_out(up)
+    pair_out(down)
+    first(4)
+    second(3)
+    lax.fori_loop(0, 16, last, None)
+    pair_out(far)
+    for zs in range(4):
+        pair_in(zs)
+    fifth(0)
+    multiply(0)
+    fourth(2)
+    third(3)
+    second(4)
+    fifth(1)
+    multiply(1)
+    fourth(3)
+    third(4)
+    fifth(2)
+    multiply(2)
+    fourth(4)
+    fifth(3)
+    multiply(3)
+    fifth(4)
+    multiply(4)
 
     for d in range(4):
         for c in range(2):
@@ -393,17 +411,23 @@
     outs = []
     for r in range(8):
         ins[r].wait()
+        lead = r * block_rows % 8
+        base, end = r * block_rows - lead, lead + block_rows
         for h in range(2):
             for t in range(TILES):
-                at = h * HALF + STARTS[t]
-                rows = min(SIZES[t], block_rows - at)
-                if rows <= 0:
-                    continue
-                code = codes[r, at : at + SIZES[t], :].astype(jnp.int32).astype(jnp.float32)
+                start = h * HALF + STARTS[t]
+                stop = min(start + SIZES[t], end)
                 line = (r % 2) * 8 + t
-                value = (code * (1.0 / TOP)) * m_ref[r // 2, h, line : line + 1, :]
-                values[r * block_rows + at : r * block_rows + at + rows, :] = value[0:rows]
-        low, high = r * block_rows // 8 * 8, (r + 1) * block_rows // 8 * 8
+                top = m_ref[r // 2, h, line : line + 1, :]
+                cuts = [max(start, lead), stop]
+                if lead and start == 0:
+                    cuts.insert(1, 8)
+                if stop % 8:
+                    cuts.insert(-1, stop // 8 * 8)
+                for a, b in zip(cuts, cuts[1:]):
+                    code = codes[r, a:b, :].astype(jnp.int32).astype(jnp.float32)
+                    values[base + a : base + b, :] = (code * (1.0 / TOP)) * top
+        low, high = base, (r + 1) * block_rows // 8 * 8
         copy = pltpu.make_async_copy(values.at[low:high], o_ref.at[low:high], out_sem.at[r])
         copy.start()
         outs.append(copy)
@@ -422,9 +446,13 @@
             jax.ShapeDtypeStruct((4, 2, 2 * HALF, 128), jnp.int16),
             jax.ShapeDtypeStruct((4, 2, 16, 128), jnp.float32),
         ),
-        in_specs=[vmem] * 3,
+        in_specs=[hbm] * 3,
         out_specs=(hbm, hbm),
         scratch_shapes=[
+            pltpu.VMEM(amplitudes.shape, bf16),
+            pltpu.VMEM(integrals.shape, bf16),
+            pltpu.VMEM((4, 128), jnp.int32),
+            dma((3,)),
             pltpu.VMEM((2 * HALF, 256), bf16),
             pltpu.VMEM((HALF, 512), bf16),
             pltpu.VMEM((512, 512), bf16),

time: 99 us -> 96.8 us (0.978)
  Pallas kernels: 98.8 us -> 96.6 us
    pallas_call x1, Pallas kernels: 94.5 us -> 92.2 us  [shards(): pl.pallas_call(ladder_kernel, out_shape=(jax.ShapeDtypeStruct((4, 2, 2 *...]
where the time goes in v4:
time: 96.8 us; the launch traced here: 96.6 us
  Pallas kernels  96.6 us (100%)
    pallas_call x1, Pallas kernels, shards(): pl.pallas_call(ladder_kernel, out_shape=(jax.ShapeDtypeStruct((4, 2, 2 *...  92.2 us
    pallas_call x1, Pallas kernels, shards(): pl.pallas_call(functools.partial(decode_kernel, rows), out_shape=jax.Shap...  4.34 us

profile of v4, /device:TPU:1, one launch (start us, length us, event | category | flops | bytes accessed | tf_op | source)
XLA Modules:
  0.0 96.6 jit_solution(17631699452487858342)
XLA Ops:
  0.0 92.2 %shard_map.37 = (s16[4,2,1280,128]{3,2,1,0:T(8,128)(2,1)}, f32[4,2,16,128]{3,2,1,0:T(8,128)}) custom-call(bf16[1250,256]{1,0:T(8,128)(2,1)} %a_hbm.1, bf16[32,16384]{1,0:T(8,128)(2,1)} %i_hbm.1, s32[4,128]{1,0:T(4,128)} %bitcast.3), custom_call_target="tpu_custom_call" | custom-call | tf_op jit(solution)/shard_map/pallas_call | solution.py:443
  92.2 4.3 %shard_map.38 = f32[10000,128]{1,0:T(8,128)} custom-call(s16[8,1280,128]{2,1,0:T(8,128)(2,1)} %bitcast.2, f32[4,2,16,128]{3,2,1,0:T(8,128)} %get-tuple-element.8.m_ref), custom_call_target="tpu_custom_call" | custom-call | tf_op jit(solution)/shard_map/pallas_call | solution.py:474

commit v5 on v4

--- a/solution.py
+++ b/solution.py
@@ -404,13 +404,9 @@
             wait(m_ref.at[zs, c], top_recv.at[zs * 2 + c])
 
 
-def decode_kernel(block_rows, q_ref, m_ref, o_ref, codes, values, in_sem, out_sem):
-    ins = [pltpu.make_async_copy(q_ref.at[r], codes.at[r], in_sem.at[r]) for r in range(8)]
-    for copy in ins:
-        copy.start()
+def decode_kernel(block_rows, q_ref, m_ref, o_ref, values, out_sem):
     outs = []
     for r in range(8):
-        ins[r].wait()
         lead = r * block_rows % 8
         base, end = r * block_rows - lead, lead + block_rows
         for h in range(2):
@@ -425,7 +421,7 @@
                 if stop % 8:
                     cuts.insert(-1, stop // 8 * 8)
                 for a, b in zip(cuts, cuts[1:]):
-                    code = codes[r, a:b, :].astype(jnp.int32).astype(jnp.float32)
+                    code = q_ref[r, a:b, :].astype(jnp.int32).astype(jnp.float32)
                     values[base + a : base + b, :] = (code * (1.0 / TOP)) * top
         low, high = base, (r + 1) * block_rows // 8 * 8
         copy = pltpu.make_async_copy(values.at[low:high], o_ref.at[low:high], out_sem.at[r])
@@ -443,11 +439,11 @@
     codes, tops = pl.pallas_call(
         ladder_kernel,
         out_shape=(
-            jax.ShapeDtypeStruct((4, 2, 2 * HALF, 128), jnp.int16),
-            jax.ShapeDtypeStruct((4, 2, 16, 128), jnp.float32),
+            pltpu.VMEM((4, 2, 2 * HALF, 128), jnp.int16),
+            pltpu.VMEM((4, 2, 16, 128), jnp.float32),
         ),
         in_specs=[hbm] * 3,
-        out_specs=(hbm, hbm),
+        out_specs=(vmem, vmem),
         scratch_shapes=[
             pltpu.VMEM(amplitudes.shape, bf16),
             pltpu.VMEM(integrals.shape, bf16),
@@ -467,21 +463,20 @@
             dma((TILES,)), dma((TILES * 32,)), dma((TILES,)), dma((8,)), dma((8,)), dma((8,)),
         ],
         compiler_params=pltpu.CompilerParams(
-            collective_id=0, has_side_effects=True, vmem_limit_bytes=56 * 2**20
+            collective_id=0, has_side_effects=True, vmem_limit_bytes=57 * 2**20
         ),
     )(amplitudes, integrals, storage_slot.reshape(4, 128))
     rows = amplitudes.shape[0]
     return pl.pallas_call(
         functools.partial(decode_kernel, rows),
         out_shape=jax.ShapeDtypeStruct((8 * rows, 128), jnp.float32),
-        in_specs=[hbm, vmem],
+        in_specs=[vmem, vmem],
         out_specs=hbm,
         scratch_shapes=[
-            pltpu.VMEM((8, 2 * HALF, 128), jnp.int16),
             pltpu.VMEM((8 * rows, 128), jnp.float32),
-            dma((8,)), dma((8,)),
+            dma((8,)),
         ],
-        compiler_params=pltpu.CompilerParams(vmem_limit_bytes=60 * 2**20),
+        compiler_params=pltpu.CompilerParams(vmem_limit_bytes=32 * 2**20),
     )(codes.reshape(8, 2 * HALF, 128), tops)
 
 

time: 96.8 us -> 94.6 us (0.977)
  Pallas kernels: 96.6 us -> 94.5 us
    pallas_call x1, Pallas kernels: 4.34 us -> 2.46 us  [shards(): pl.pallas_call(functools.partial(decode_kernel, rows), out_shape=jax.Shap...]
where the time goes in v5:
time: 94.6 us; the launch traced here: 94.5 us
  Pallas kernels  94.5 us (100%)
    pallas_call x1, Pallas kernels, shards(): pl.pallas_call(ladder_kernel, out_shape=(pltpu.VMEM((4, 2, 2 * HALF, 128)...  92 us
    pallas_call x1, Pallas kernels, shards(): pl.pallas_call(functools.partial(decode_kernel, rows), out_shape=jax.Shap...  2.46 us

profile of v5, /device:TPU:1, one launch (start us, length us, event | category | flops | bytes accessed | tf_op | source)
XLA Modules:
  0.0 94.5 jit_solution(4841048072876727853)
XLA Ops:
  0.0 92.0 %shard_map.37 = (s16[4,2,1280,128]{3,2,1,0:T(8,128)(2,1)S(1)}, f32[4,2,16,128]{3,2,1,0:T(8,128)S(1)}) custom-call(bf16[1250,256]{1,0:T(8,128)(2,1)} %a_hbm.1, bf16[32,16384]{1,0:T(8,128)(2,1)} %i_hbm.1, s32[4,128]{1,0:T(4,128)} %bitcast.3), custom_call_target="tpu_custom_call" | custom-call | tf_op jit(solution)/shard_map/pallas_call | solution.py:439
  92.1 2.5 %shard_map.38 = f32[10000,128]{1,0:T(8,128)} custom-call(s16[8,1280,128]{2,1,0:T(8,128)(2,1)S(1)} %bitcast.2, f32[4,2,16,128]{3,2,1,0:T(8,128)S(1)} %get-tuple-element.8.m_ref), custom_call_target="tpu_custom_call" | custom-call | tf_op jit(solution)/shard_map/pallas_call | solution.py:470

commit v6 on v5

--- a/solution.py
+++ b/solution.py
@@ -335,10 +335,10 @@
     second(2)
     relays(sources[6:16])
     fourth(1)
-    third(2)
     lax.fori_loop(0, 16, rest, None)
     pair_out(up)
     pair_out(down)
+    third(2)
     first(4)
     second(3)
     lax.fori_loop(0, 16, last, None)

time: 94.6 us -> 93.3 us (0.986)
  Pallas kernels: 94.5 us -> 93.2 us
    pallas_call x1, Pallas kernels: 92 us -> 90.7 us  [shards(): pl.pallas_call(ladder_kernel, out_shape=(pltpu.VMEM((4, 2, 2 * HALF, 128)...]
where the time goes in v6:
time: 93.3 us; the launch traced here: 93.2 us
  Pallas kernels  93.2 us (100%)
    pallas_call x1, Pallas kernels, shards(): pl.pallas_call(ladder_kernel, out_shape=(pltpu.VMEM((4, 2, 2 * HALF, 128)...  90.7 us
    pallas_call x1, Pallas kernels, shards(): pl.pallas_call(functools.partial(decode_kernel, rows), out_shape=jax.Shap...  2.46 us

profile of v6, /device:TPU:1, one launch (start us, length us, event | category | flops | bytes accessed | tf_op | source)
XLA Modules:
  0.0 93.2 jit_solution(10104046597412059792)
XLA Ops:
  0.0 90.7 %shard_map.37 = (s16[4,2,1280,128]{3,2,1,0:T(8,128)(2,1)S(1)}, f32[4,2,16,128]{3,2,1,0:T(8,128)S(1)}) custom-call(bf16[1250,256]{1,0:T(8,128)(2,1)} %a_hbm.1, bf16[32,16384]{1,0:T(8,128)(2,1)} %i_hbm.1, s32[4,128]{1,0:T(4,128)} %bitcast.3), custom_call_target="tpu_custom_call" | custom-call | tf_op jit(solution)/shard_map/pallas_call | solution.py:439
  90.7 2.5 %shard_map.38 = f32[10000,128]{1,0:T(8,128)} custom-call(s16[8,1280,128]{2,1,0:T(8,128)(2,1)S(1)} %bitcast.2, f32[4,2,16,128]{3,2,1,0:T(8,128)S(1)} %get-tuple-element.8.m_ref), custom_call_target="tpu_custom_call" | custom-call | tf_op jit(solution)/shard_map/pallas_call | solution.py:470

commit v7 on v6

--- a/solution.py
+++ b/solution.py
@@ -144,7 +144,7 @@
                 device_id=device(px, py, z, k), device_id_type=MESH,
             ).start()
 
-    plane_out(STEPS[:8])
+    plane_out(STEPS)
     line_copy(z, me, up)
     line_copy(z, me, down)
 
@@ -314,7 +314,6 @@
 
     order(0)
     first(0)
-    plane_out(STEPS[8:])
     order(1)
     first(1)
     plane_in(sources[1:8])
@@ -339,8 +338,8 @@
     pair_out(up)
     pair_out(down)
     third(2)
+    second(3)
     first(4)
-    second(3)
     lax.fori_loop(0, 16, last, None)
     pair_out(far)
     for zs in range(4):

time: 93.3 us -> 92.7 us (level)
  no operation moved by 1% of the time
where the time goes in v7:
time: 92.7 us; the launch traced here: 92.6 us
  Pallas kernels  92.6 us (100%)
    pallas_call x1, Pallas kernels, shards(): pl.pallas_call(ladder_kernel, out_shape=(pltpu.VMEM((4, 2, 2 * HALF, 128)...  90.1 us
    pallas_call x1, Pallas kernels, shards(): pl.pallas_call(functools.partial(decode_kernel, rows), out_shape=jax.Shap...  2.46 us

profile of v7, /device:TPU:1, one launch (start us, length us, event | category | flops | bytes accessed | tf_op | source)
XLA Modules:
  0.0 92.6 jit_solution(3593081635514635010)
XLA Ops:
  0.0 90.1 %shard_map.37 = (s16[4,2,1280,128]{3,2,1,0:T(8,128)(2,1)S(1)}, f32[4,2,16,128]{3,2,1,0:T(8,128)S(1)}) custom-call(bf16[1250,256]{1,0:T(8,128)(2,1)} %a_hbm.1, bf16[32,16384]{1,0:T(8,128)(2,1)} %i_hbm.1, s32[4,128]{1,0:T(4,128)} %bitcast.3), custom_call_target="tpu_custom_call" | custom-call | tf_op jit(solution)/shard_map/pallas_call | solution.py:438
  90.1 2.5 %shard_map.38 = f32[10000,128]{1,0:T(8,128)} custom-call(s16[8,1280,128]{2,1,0:T(8,128)(2,1)S(1)} %bitcast.2, f32[4,2,16,128]{3,2,1,0:T(8,128)S(1)} %get-tuple-element.8.m_ref), custom_call_target="tpu_custom_call" | custom-call | tf_op jit(solution)/shard_map/pallas_call | solution.py:469

commit v8 on v7

--- a/solution.py
+++ b/solution.py
@@ -277,7 +277,7 @@
         size, start = SIZES[t], STARTS[t]
 
         def one(n, _):
-            to = (z + 2 + 3 * n) & 3
+            to = (z + 2 + 3 * n + (n >> 1) * (3 - 2 * (n & 1))) & 3
             total = jnp.dot(
                 amp[2 * start : 2 * (start + size), :],
                 ints[:, pl.ds(pl.multiple_of(to * 256, 256), 256)],

time: 92.7 us -> 92.7 us (level)
  no operation moved by 1% of the time
where the time goes in v8:
time: 92.7 us; the launch traced here: 92.6 us
  Pallas kernels  92.6 us (100%)
    pallas_call x1, Pallas kernels, shards(): pl.pallas_call(ladder_kernel, out_shape=(pltpu.VMEM((4, 2, 2 * HALF, 128)...  90.1 us
    pallas_call x1, Pallas kernels, shards(): pl.pallas_call(functools.partial(decode_kernel, rows), out_shape=jax.Shap...  2.46 us

profile of v8, /device:TPU:1, one launch (start us, length us, event | category | flops | bytes accessed | tf_op | source)
XLA Modules:
  0.0 92.6 jit_solution(3913141426999739775)
XLA Ops:
  0.0 90.1 %shard_map.37 = (s16[4,2,1280,128]{3,2,1,0:T(8,128)(2,1)S(1)}, f32[4,2,16,128]{3,2,1,0:T(8,128)S(1)}) custom-call(bf16[1250,256]{1,0:T(8,128)(2,1)} %a_hbm.1, bf16[32,16384]{1,0:T(8,128)(2,1)} %i_hbm.1, s32[4,128]{1,0:T(4,128)} %bitcast.3), custom_call_target="tpu_custom_call" | custom-call | tf_op jit(solution)/shard_map/pallas_call | solution.py:438
  90.1 2.5 %shard_map.38 = f32[10000,128]{1,0:T(8,128)} custom-call(s16[8,1280,128]{2,1,0:T(8,128)(2,1)S(1)} %bitcast.2, f32[4,2,16,128]{3,2,1,0:T(8,128)S(1)} %get-tuple-element.8.m_ref), custom_call_target="tpu_custom_call" | custom-call | tf_op jit(solution)/shard_map/pallas_call | solution.py:469
